TPU v7x, 512 devices: a whole 4x8x8 slice. The times are simulated.
512 devices in a mesh: pipe: 8 (over x, core), expert: 64 (over y, z).
Axes of the slice: x: 4, y: 8, z: 8, core: 2. Of those that a mesh axis runs over, the one named last changes fastest.
Arguments:
- fwd_tokens: bfloat16 [4096, 7168], P('expert', 'pipe'), may hold values from -6 to 6
- fwd_ids: int32 [4096, 8], P('expert'), may hold values from 0 to 63, all different within a row; in each aligned block of 64 rows (0 to 63, 64 to 127, ...) at most 10 rows name the same one
- fwd_gates: float32 [4096, 8], P('expert'), may hold values from 0.2 to 1
- bwd_tokens: bfloat16 [4096, 7168], P('expert', 'pipe'), may hold values from -6 to 6
- bwd_ids: int32 [4096, 8], P('expert'), may hold values from 0 to 63, all different within a row; in each aligned block of 64 rows (0 to 63, 64 to 127, ...) at most 10 rows name the same one
- bwd_gates: float32 [4096, 8], P('expert'), may hold values from 0.2 to 1
- bwd_cotangent: bfloat16 [4096, 7168], P('expert', 'pipe'), may hold values from -6 to 6
- w_up: bfloat16 [64, 7168, 1024], P('expert', 'pipe'), may hold values from -0.0625 to 0.0625
- w_down: bfloat16 [64, 1024, 7168], P('expert', None, 'pipe'), may hold values from -0.1875 to 0.1875
Outputs:
- fwd_out: bfloat16 [4096, 7168], P('expert', 'pipe')
- grad_in: bfloat16 [4096, 7168], P('expert', 'pipe')
Inputs may be any that keep to these rules, and one draw needn't show every extreme that they name: `fwd_ids`: in the 64 rows of one device no expert is named by more than 10 rows, a bound that some block reaches; a row names 8 different experts. `bwd_ids`: in the 64 rows of one device no expert is named by more than 10 rows, a bound that some block reaches; a row names 8 different experts.
All inputs are finite; a program needn't handle non-finite values.
Results may differ from a plain program's by a relative error of at most 0.025.
Values may be sent and summed in bfloat16 or wider, within the bound.
A program may use at most 64 MiB of HBM per device.

v0:
```python
import jax
import jax.numpy as jnp
from jax import lax
from jax.sharding import PartitionSpec as P


def for_sending(array):
    return jax.tree.map(lambda a: a.astype(jnp.bfloat16) if a.dtype == jnp.float32 else a, array)


def routing(ids, experts_here, capacity):
    token_rows, top_count = ids.shape
    flat_ids = ids.reshape(-1)
    labels = jnp.arange(experts_here, dtype=jnp.int32)
    onehot = (flat_ids[:, None] == labels[None, :]).astype(jnp.int32)
    rank_in = jnp.sum((jnp.cumsum(onehot, axis=0) - 1) * onehot, axis=1)
    slot_of = flat_ids * capacity + rank_in
    positions = jnp.arange(experts_here * capacity, dtype=jnp.int32)
    picks = (slot_of[:, None] == positions[None, :]).astype(jnp.bfloat16)
    selector = jnp.sum(picks.reshape(token_rows, top_count, -1), axis=1).T
    return (selector, slot_of.reshape(token_rows, top_count))


def pick_rows(selector, tokens):
    return jnp.dot(selector, tokens, preferred_element_type=jnp.float32).astype(jnp.bfloat16)


def rounded(value):
    return value.astype(jnp.bfloat16).astype(jnp.float32)


def local(
    fwd_tokens, fwd_ids, fwd_gates, bwd_tokens, bwd_ids, bwd_gates, bwd_cotangent, w_up, w_down
):
    experts_here = lax.axis_size("expert")
    column_share = fwd_tokens.shape[1]
    capacity = max(2, 5 * fwd_ids.shape[0] * fwd_ids.shape[1] // (4 * experts_here))
    slot_count = experts_here * capacity
    up_local = w_up[0]
    down_local = w_down[0]
    fwd_select, fwd_slot = routing(fwd_ids, experts_here, capacity)
    bwd_select, bwd_slot = routing(bwd_ids, experts_here, capacity)
    contract_last = (((1,), (1,)), ((), ()))

    def arrive(sources, selector):
        pieces = tuple(
            (pick_rows(selector, v).reshape(experts_here, capacity, column_share) for v in sources)
        )
        received = jax.tree.map(
            lambda part, own: part.astype(own.dtype),
            lax.all_to_all(for_sending(pieces), "expert", split_axis=0, concat_axis=0, tiled=True),
            pieces,
        )
        return tuple((v.reshape(slot_count, column_share) for v in received))

    def middle(terms, finish):
        sums = jax.tree.map(
            lambda part: part.astype(jnp.float32), lax.psum(for_sending(terms), "pipe")
        )
        return finish(sums)

    def depart(results, slot_of, gates):
        returned = lax.all_to_all(
            results.reshape(experts_here, capacity, column_share),
            "expert",
            split_axis=0,
            concat_axis=0,
            tiled=True,
        )
        picked = returned.reshape(slot_count, column_share)[slot_of].astype(jnp.float32)
        return jnp.sum(gates[:, :, None] * picked, axis=1).astype(jnp.bfloat16)

    def finish_forward(sums):
        return jax.nn.silu(sums[0]).astype(jnp.bfloat16)

    def finish_backward(sums):
        pre_act, dact = sums
        sigma = jax.nn.sigmoid(pre_act)
        return (dact * sigma * (1.0 + pre_act * (1.0 - sigma))).astype(jnp.bfloat16)

    (fwd_rows,) = arrive((fwd_tokens,), fwd_select)
    fwd_term = rounded(jnp.dot(fwd_rows, up_local, preferred_element_type=jnp.float32))
    fwd_act = middle((fwd_term,), finish_forward)
    fwd_res = jnp.dot(fwd_act, down_local, preferred_element_type=jnp.float32).astype(jnp.bfloat16)
    bwd_rows, bwd_grads = arrive((bwd_tokens, bwd_cotangent), bwd_select)
    pre_term = rounded(jnp.dot(bwd_rows, up_local, preferred_element_type=jnp.float32))
    dact_term = rounded(
        lax.dot_general(bwd_grads, down_local, contract_last, preferred_element_type=jnp.float32)
    )
    bwd_dpre = middle((pre_term, dact_term), finish_backward)
    bwd_res = lax.dot_general(
        bwd_dpre, up_local, contract_last, preferred_element_type=jnp.float32
    ).astype(jnp.bfloat16)
    fwd_out = depart(fwd_res, fwd_slot, fwd_gates)
    grad_in = depart(bwd_res, bwd_slot, bwd_gates)
    return (fwd_out, grad_in)


def solution(mesh):
    in_specs = (
        P("expert", "pipe"),
        P("expert", None),
        P("expert", None),
        P("expert", "pipe"),
        P("expert", None),
        P("expert", None),
        P("expert", "pipe"),
        P("expert", "pipe", None),
        P("expert", None, "pipe"),
    )
    out_specs = (P("expert", "pipe"), P("expert", "pipe"))
    return jax.shard_map(local, mesh=mesh, in_specs=in_specs, out_specs=out_specs, check_vma=False)
```

profile of v0, /device:TPU:6, one launch (start us, length us, event | category | flops | bytes accessed | tf_op | source)
XLA Modules:
  0.0 406.3 jit_solution(3707707055198686332)
XLA Ops:
  7.2 0.9 copy.47
  8.1 0.1 eq.93
  8.3 1.2 reduce-window.16
  9.5 0.2 slice_reduce_fusion
  9.8 0.1 fusion.45
  10.0 0.7 compare_select_fusion
  10.8 0.5 fusion.42
  11.3 1.4 convolution_convert_fusion
  12.7 1.5 reshape.122
  14.2 16.9 %all-to-all-start.3 = ((bf16[64,10,896]{2,1,0:T(8,128)(2,1)}), bf16[64,10,896]{2,1,0:T(8,128)(2,1)}, u32[]{:S(2)}, u32[]{:S(2)}) async-start(bf16[64,10,896]{2,1,0:T(8,128)(2,1)} %reshape.122), calls=%async_computation.3 | async-start | bytes 3670016 | tf_op jit(solution)/shard_map/all_to_all | solution.py:51
  31.2 0.1 eq.82
  31.4 1.2 reduce-window.14
  32.6 0.2 slice_reduce_fusion.1
  32.9 0.1 fusion.47
  33.3 0.5 fusion.43
  33.7 0.5 convolution_convert_fusion.2
  34.2 1.4 reshape.115
  35.7 41.7 %all-to-all-done.3 = bf16[64,10,896]{2,1,0:T(8,128)(2,1)} async-done(((bf16[64,10,896]{2,1,0:T(8,128)(2,1)}), bf16[64,10,896]{2,1,0:T(8,128)(2,1)}, u32[]{:S(2)}, u32[]{:S(2)}) %all-to-all-start.3) | async-done | bytes 1146912 | tf_op jit(solution)/shard_map/all_to_all | solution.py:51
  77.3 10.1 %all-to-all-start = ((bf16[64,10,896]{2,1,0:T(8,128)(2,1)}), bf16[64,10,896]{2,1,0:T(8,128)(2,1)}, u32[]{:S(2)}, u32[]{:S(2)}) async-start(bf16[64,10,896]{2,1,0:T(8,128)(2,1)} %reshape.115), calls=%async_computation | async-start | bytes 3670016 | tf_op jit(solution)/shard_map/all_to_all | solution.py:51
  87.5 0.5 convolution_convert_fusion.1
  88.0 1.5 reshape.120
  89.4 42.9 %all-to-all-done = bf16[64,10,896]{2,1,0:T(8,128)(2,1)} async-done(((bf16[64,10,896]{2,1,0:T(8,128)(2,1)}), bf16[64,10,896]{2,1,0:T(8,128)(2,1)}, u32[]{:S(2)}, u32[]{:S(2)}) %all-to-all-start) | async-done | bytes 1146912 | tf_op jit(solution)/shard_map/all_to_all | solution.py:51
  132.4 8.8 %all-to-all-start.2 = ((bf16[64,10,896]{2,1,0:T(8,128)(2,1)}), bf16[64,10,896]{2,1,0:T(8,128)(2,1)}, u32[]{:S(2)}, u32[]{:S(2)}) async-start(bf16[64,10,896]{2,1,0:T(8,128)(2,1)} %reshape.120), calls=%async_computation.2 | async-start | bytes 3670016 | tf_op jit(solution)/shard_map/all_to_all | solution.py:51
  141.2 0.2 all-reduce.3.cloned.1.call-start
  141.4 2.4 reshape.123
  143.8 3.5 reshape.116
  147.3 2.6 fusion.25
  149.9 2.6 fusion.22
  152.5 32.2 %all-to-all-done.2 = bf16[64,10,896]{2,1,0:T(8,128)(2,1)} async-done(((bf16[64,10,896]{2,1,0:T(8,128)(2,1)}), bf16[64,10,896]{2,1,0:T(8,128)(2,1)}, u32[]{:S(2)}, u32[]{:S(2)}) %all-to-all-start.2) | async-done | bytes 1146912 | tf_op jit(solution)/shard_map/all_to_all | solution.py:51
  184.8 2.4 reshape.121
  187.2 4.2 %fusion.28 = bf16[640,1024]{1,0:T(8,128)(2,1)} fusion(bf16[640,896]{1,0:T(8,128)(2,1)S(1)} %reshape.121, bf16[1,1024,896]{2,1,0:T(8,128)(2,1)} %param.17), kind=kOutput, calls=%fused_computation.32 | convolution fusion | flops 1175060480 | bytes 4292608 | tf_op jit(solution)/shard_map/dot_general | solution.py:88
  191.4 77.2 %all-reduce.3.cloned.1.call-done = (bf16[640,1024]{1,0:T(8,128)(2,1)}, bf16[640,1024]{1,0:T(8,128)(2,1)}, bf16[640,1024]{1,0:T(8,128)(2,1)}) async-done(((bf16[640,1024]{1,0:T(8,128)(2,1)}, bf16[640,1024]{1,0:T(8,128)(2,1)}, bf16[640,1024]{1,0:T(8,128)(2,1)}), (bf16[640,1024]{1,0:T(8,128)(2,1)}, bf16[640,1024]{1,0:T(8,128)(2,1)}, bf16[640,1024]{1,0:T(8,128)(2,1)})) %all-reduce.3.cloned.1.call-update) | async-done | bytes 3932176 | tf_op jit(solution)/shard_map/psum | solution.py:58
  268.6 3.7 fusion.31
  272.3 1.4 reshape.124
  273.7 13.5 %all-to-all-start.4 = ((bf16[64,10,896]{2,1,0:T(8,128)(2,1)}), bf16[64,10,896]{2,1,0:T(8,128)(2,1)}, u32[]{:S(2)}, u32[]{:S(2)}) async-start(bf16[64,10,896]{2,1,0:T(8,128)(2,1)} %reshape.124), calls=%async_computation.4 | async-start | bytes 3670016 | tf_op jit(solution)/shard_map/all_to_all | solution.py:63
  287.2 3.4 fusion.34
  290.7 1.5 reshape.117
  292.2 40.1 %all-to-all-done.4 = bf16[64,10,896]{2,1,0:T(8,128)(2,1)} async-done(((bf16[64,10,896]{2,1,0:T(8,128)(2,1)}), bf16[64,10,896]{2,1,0:T(8,128)(2,1)}, u32[]{:S(2)}, u32[]{:S(2)}) %all-to-all-start.4) | async-done | bytes 1146912 | tf_op jit(solution)/shard_map/all_to_all | solution.py:63
  332.3 13.2 %all-to-all-start.1 = ((bf16[64,10,896]{2,1,0:T(8,128)(2,1)}), bf16[64,10,896]{2,1,0:T(8,128)(2,1)}, u32[]{:S(2)}, u32[]{:S(2)}) async-start(bf16[64,10,896]{2,1,0:T(8,128)(2,1)} %reshape.117), calls=%async_computation.1 | async-start | bytes 3670016 | tf_op jit(solution)/shard_map/all_to_all | solution.py:63
  345.6 0.1 reshape.136
  345.9 0.1 reshape.128
  346.1 2.4 reshape.125
  348.5 2.7 gather_fusion.1
  351.3 2.4 fusion.10
  353.7 38.1 %all-to-all-done.1 = bf16[64,10,896]{2,1,0:T(8,128)(2,1)} async-done(((bf16[64,10,896]{2,1,0:T(8,128)(2,1)}), bf16[64,10,896]{2,1,0:T(8,128)(2,1)}, u32[]{:S(2)}, u32[]{:S(2)}) %all-to-all-start.1) | async-done | bytes 1146912 | tf_op jit(solution)/shard_map/all_to_all | solution.py:63
  391.8 2.4 reshape.118
  394.3 2.8 gather_fusion
  397.0 2.4 fusion.11
  (37 shorter events, 1.2 us)
Async XLA Ops:
  7.2 140.1 %copy-start = (bf16[1,896,1024]{2,1,0:T(8,128)(2,1)S(1)}, bf16[1,896,1024]{2,1,0:T(8,128)(2,1)}, u32[]{:S(2)}) copy-start(bf16[1,896,1024]{2,1,0:T(8,128)(2,1)} %param.16) | copy-start | bytes 5505028
  14.1 17.0 %copy-start.4 = (s32[64,8]{0,1:T(8,128)S(1)}, s32[64,8]{0,1:T(8,128)}, u32[]{:S(2)}) copy-start(s32[64,8]{0,1:T(8,128)} %param.10) | copy-start | bytes 6148
  14.2 19.6 %copy-start.2 = (bf16[64,896]{1,0:T(8,128)(2,1)S(1)}, bf16[64,896]{1,0:T(8,128)(2,1)}, u32[]{:S(2)}) copy-start(bf16[64,896]{1,0:T(8,128)(2,1)} %param.9) | copy-start | bytes 344068
  14.2 63.2 %all-to-all-start.3 = ((bf16[64,10,896]{2,1,0:T(8,128)(2,1)}), bf16[64,10,896]{2,1,0:T(8,128)(2,1)}, u32[]{:S(2)}, u32[]{:S(2)}) async-start(bf16[64,10,896]{2,1,0:T(8,128)(2,1)} %reshape.122), calls=%async_computation.3 | async-start | bytes 3670016 | tf_op jit(solution)/shard_map/all_to_all | solution.py:51
  35.7 51.8 %copy-start.3 = (bf16[64,896]{1,0:T(8,128)(2,1)S(1)}, bf16[64,896]{1,0:T(8,128)(2,1)}, u32[]{:S(2)}) copy-start(bf16[64,896]{1,0:T(8,128)(2,1)} %param.15) | copy-start | bytes 344068
  77.3 55.0 %all-to-all-start = ((bf16[64,10,896]{2,1,0:T(8,128)(2,1)}), bf16[64,10,896]{2,1,0:T(8,128)(2,1)}, u32[]{:S(2)}, u32[]{:S(2)}) async-start(bf16[64,10,896]{2,1,0:T(8,128)(2,1)} %reshape.115), calls=%async_computation | async-start | bytes 3670016 | tf_op jit(solution)/shard_map/all_to_all | solution.py:51
  132.4 52.4 %all-to-all-start.2 = ((bf16[64,10,896]{2,1,0:T(8,128)(2,1)}), bf16[64,10,896]{2,1,0:T(8,128)(2,1)}, u32[]{:S(2)}, u32[]{:S(2)}) async-start(bf16[64,10,896]{2,1,0:T(8,128)(2,1)} %reshape.120), calls=%async_computation.2 | async-start | bytes 3670016 | tf_op jit(solution)/shard_map/all_to_all | solution.py:51
  141.2 127.4 %all-reduce.3.cloned.1.call-start = ((), (), s32[]{:S(2)}) async-start(), calls=%async_computation.5 | async-start | bytes 7864320 | tf_op jit(solution)/shard_map/psum | solution.py:58
  147.3 2.6 copy-start.1
  273.7 58.6 %all-to-all-start.4 = ((bf16[64,10,896]{2,1,0:T(8,128)(2,1)}), bf16[64,10,896]{2,1,0:T(8,128)(2,1)}, u32[]{:S(2)}, u32[]{:S(2)}) async-start(bf16[64,10,896]{2,1,0:T(8,128)(2,1)} %reshape.124), calls=%async_computation.4 | async-start | bytes 3670016 | tf_op jit(solution)/shard_map/all_to_all | solution.py:63
  292.1 53.6 %copy-start.5 = (f32[64,8]{0,1:T(8,128)S(1)}, f32[64,8]{0,1:T(8,128)}, u32[]{:S(2)}) copy-start(f32[64,8]{0,1:T(8,128)} %param.14) | copy-start | bytes 6148
  292.2 53.8 %copy-start.6 = (f32[64,8]{0,1:T(8,128)S(1)}, f32[64,8]{0,1:T(8,128)}, u32[]{:S(2)}) copy-start(f32[64,8]{0,1:T(8,128)} %param.11) | copy-start | bytes 6148
  332.3 59.6 %all-to-all-start.1 = ((bf16[64,10,896]{2,1,0:T(8,128)(2,1)}), bf16[64,10,896]{2,1,0:T(8,128)(2,1)}, u32[]{:S(2)}, u32[]{:S(2)}) async-start(bf16[64,10,896]{2,1,0:T(8,128)(2,1)} %reshape.117), calls=%async_computation.1 | async-start | bytes 3670016 | tf_op jit(solution)/shard_map/all_to_all | solution.py:63
Sparse Core Ops, SparseCore 0:
  191.5 76.9 all-reduce.2
where the time goes:
time: 411 us; the launch traced here: 406 us
  waiting for transfers between devices  272 us (66%)
  starting transfers between devices  62.8 us (15%)
  local copies, waits for them, and re-layouts  28.7 us (7%)
  matrix products  19 us (5%)
  between operations  14.3 us (3%)
  other arithmetic  9.3 us (2%)
    all_to_all x3, waiting for transfers between devices, arrive(): lax.all_to_all(for_sending(pieces), 'expert', split_axis=0, concat_axis=0...  117 us
    all_to_all x2, waiting for transfers between devices, depart(): lax.all_to_all(results.reshape(experts_here, capacity, column_share), 'ex...  78.3 us
    psum x1, waiting for transfers between devices, middle(): lax.psum(for_sending(terms), 'pipe')  77.2 us
    all_to_all x3, starting transfers between devices, arrive(): lax.all_to_all(for_sending(pieces), 'expert', split_axis=0, concat_axis=0...  35.8 us
    all_to_all x2, starting transfers between devices, depart(): lax.all_to_all(results.reshape(experts_here, capacity, column_share), 'ex...  26.8 us
    reshape x3, local copies, waits for them, and re-layouts, arrive(): return tuple((v.reshape(slot_count, column_share) for v in received))  8.32 us
  transfers between devices with their start and end apart: 6, of which 6 were waited for; matrix products, arithmetic and copies ran while one was open for 8% of the time, Pallas kernels for 0%

commit v1 on v0

v1 whole, which is shorter than its diff:
```python
import functools
import math

import jax
import jax.numpy as jnp
from jax import lax
from jax.experimental import pallas as pl
from jax.experimental.pallas import tpu as pltpu
from jax.sharding import PartitionSpec as P

MESH = pl.DeviceIdType.MESH
F32 = jnp.float32
BF16 = jnp.bfloat16
NN = (((1,), (0,)), ((), ()))
NT = (((1,), (1,)), ((), ()))
TN = (((0,), (0,)), ((), ()))


def dot(left, right, dims=NN):
    return lax.dot_general(left, right, dims, preferred_element_type=F32)


def column_tiles(width, tile, body):
    whole = width // tile

    def step(index, carry):
        body(pl.multiple_of(index * tile, tile), tile)
        return carry

    if whole:
        lax.fori_loop(0, whole, step, 0)
    if width % tile:
        body(whole * tile, width % tile)


def kernel(
    side, nx, chunks, tile,
    ft, fi, fg, bt, bi, bg, bc, wu_hbm, wd_hbm,
    fwd_out, grad_out,
    wu, wd, ids, ids_t, info_own, info_all, slots, sel, gsel, perm,
    gathered, sending, arrived, kept, pair_tmp, pair_out, pair_in, xsend, xrecv,
    act, res_acc, res, returned, partial, part_send, part_recv,
    lsem, info_s, info_r, gat_s, gat_r, a2a_s, a2a_r, pr1_s, pr1_r, xrs_s, xrs_r,
    xag_s, xag_r, pr2_s, pr2_r, ret_s, ret_r, red_s, red_r,
):
    tok = ft.shape[0]
    half = wu.shape[1] // 2
    p = lax.axis_index("pipe")
    e = lax.axis_index("expert")
    x, c = p // 2, p % 2
    y, z = e // side, e % side
    j = z + c * (y - z)
    m = y + c * (z - y)
    sj = 1 + c * (side - 1)
    sm = side - c * (side - 1)

    def around(place, step, size):
        return (place + step) % size

    def gather_dev(place):
        return (p, place * sj + m * sm)

    def row_dev(place):
        return (p, j * sj + place * sm)

    def x_dev(place):
        return (place * 2 + c, e)

    core_dev = (x * 2 + 1 - c, e)

    def loop(start, stop, body):
        def step(index, carry):
            body(index)
            return carry

        lax.fori_loop(start, stop, step, 0)

    def remote(src, dst, ssem, rsem, device):
        return pltpu.make_async_remote_copy(
            src_ref=src, dst_ref=dst, send_sem=ssem, recv_sem=rsem,
            device_id=device, device_id_type=MESH,
        )

    tokens = (ft, bt, bc)
    route_of = (0, 1, 1)

    def own_block(q):
        return pltpu.make_async_copy(tokens[q], gathered.at[q, pl.ds(j * tok, tok)], lsem.at[q])

    load_up = pltpu.make_async_copy(wu_hbm, wu, lsem.at[3])
    load_down = pltpu.make_async_copy(wd_hbm, wd, lsem.at[4])
    for q in range(3):
        own_block(q).start()
    load_up.start()
    load_down.start()

    barrier = pltpu.get_barrier_semaphore()
    for step in range(1, side):
        pl.semaphore_signal(barrier, inc=1, device_id=gather_dev(around(j, step, side)), device_id_type=MESH)
        pl.semaphore_signal(barrier, inc=1, device_id=row_dev(around(m, step, side)), device_id_type=MESH)
    for step in range(1, nx):
        pl.semaphore_signal(barrier, inc=1, device_id=x_dev(around(x, step, nx)), device_id_type=MESH)
    pl.semaphore_signal(barrier, inc=1, device_id=core_dev, device_id_type=MESH)
    pl.semaphore_wait(barrier, 2 * (side - 1) + nx)

    def gather_copy(q, k):
        here = gathered.at[q, pl.ds(j * tok, tok)]
        return remote(tokens[q], here, gat_s.at[q, k], gat_r.at[q, k], gather_dev(around(j, k, side)))

    def info_copy(r, k):
        there = around(j, k, side)
        return remote(
            info_own.at[r, pl.ds(there * side, side)], info_all.at[r, pl.ds(j * side, side)],
            info_s.at[r, k], info_r.at[r, k], gather_dev(there),
        )

    def rows_at(n, place):
        first, count = chunks[n]
        return pl.ds(pl.multiple_of(side * first + place * count, 16), count)

    def row_copy(q, n, k):
        there = around(m, k, side)
        return remote(
            sending.at[q, rows_at(n, there)], arrived.at[q, rows_at(n, m)],
            a2a_s.at[q, n, k], a2a_r.at[q, n, k], row_dev(there),
        )

    def return_copy(r, n, k):
        there = around(m, k, side)
        return remote(
            res.at[r, rows_at(n, there)], returned.at[r, rows_at(n, m)],
            ret_s.at[r, n, k], ret_r.at[r, n, k], row_dev(there),
        )

    def reduce_copy(r, k):
        there = around(j, k, side)
        return remote(
            part_send.at[r, pl.ds(there * tok, tok)], part_recv.at[r, pl.ds(j * tok, tok)],
            red_s.at[r, k], red_r.at[r, k], gather_dev(there),
        )

    def all_rows(n):
        first, count = chunks[n]
        return pl.ds(side * first, side * count)

    def share(n, place):
        first, count = chunks[n]
        size = side * count // nx
        return pl.ds(pl.multiple_of(side * first + place * size, 16), size)

    def pair_copy(q, n):
        return remote(
            pair_out.at[q, all_rows(n)], pair_in.at[q, all_rows(n)],
            pr1_s.at[q, n], pr1_r.at[q, n], core_dev,
        )

    def scatter_copy(q, n, k):
        there = around(x, k, nx)
        return remote(
            xsend.at[q, share(n, there)], xrecv.at[q, share(n, x)],
            xrs_s.at[q, n, k], xrs_r.at[q, n, k], x_dev(there),
        )

    def spread_copy(r, n, k):
        here = act.at[r, c, share(n, x)]
        return remote(here, here, xag_s.at[r, n, k], xag_r.at[r, n, k], x_dev(around(x, k, nx)))

    def pair_act_copy(r, n):
        here = act.at[r, c, all_rows(n)]
        return remote(here, here, pr2_s.at[r, n], pr2_r.at[r, n], core_dev)

    def start_ring(size, copy):
        loop(1, size, lambda k: copy(k).start())

    def await_ring(size, copy):
        loop(1, size, lambda k: copy(k).wait_recv())

    def drain_ring(size, copy):
        loop(1, size, lambda k: copy(k).wait_send())

    def start_gather(q):
        start_ring(side, functools.partial(gather_copy, q))

    def route_info():
        rows = ids.shape[0]
        ids[...] = jnp.zeros_like(ids)
        for at in (0, rows // 2):
            for place, ref in enumerate((fi, fg, bi, bg)):
                width = ref.shape[1]
                ids[at:at + tok, place * width:(place + 1) * width] = ref[...].astype(F32)
        ids_t[...] = ids[...].T
        top = fi.shape[1]
        shape = (side * side, 2 * tok)
        row = lax.broadcasted_iota(jnp.int32, shape, 0)
        lane = lax.broadcasted_iota(jnp.int32, shape, 1)
        expert = ((row // side) * sj + (row % side) * sm).astype(F32)
        wide = (2 * tok, 2 * tok)
        before = lax.broadcasted_iota(jnp.int32, wide, 0)
        after = lax.broadcasted_iota(jnp.int32, wide, 1)
        earlier = jnp.where((before < after) & (after < tok), 1.0, 0.0).astype(BF16)
        for r in range(2):
            named = jnp.zeros(shape, F32)
            gate = jnp.zeros(shape, F32)
            for k in range(top):
                at = 2 * top * r + k
                hit = ids_t[at:at + 1, :] == expert
                named = named + jnp.where(hit, 1.0, 0.0)
                gate = gate + jnp.where(hit, ids_t[at + top:at + top + 1, :], 0.0)
            rank = dot(named.astype(BF16), earlier)
            slot = jnp.where(named > 0.5, rank * side + j.astype(F32), -1.0)
            info_own[r] = jnp.where(lane < tok, slot, gate)
            here = pl.ds(j * side, side)
            info_all[r, here] = info_own[r, here]

    def build_select(r):
        await_ring(side, functools.partial(info_copy, r))
        for b in range(side):
            here = info_all[r, b * side:(b + 1) * side, :]
            slots[0, :, b * tok:(b + 1) * tok] = here[:, :tok]
            slots[1, :, b * tok:(b + 1) * tok] = here[:, tok:]
        for n, (first, count) in enumerate(chunks):
            def body(place):
                line = lax.broadcasted_iota(jnp.int32, (count, side * tok), 0) + first
                hit = slots[0, pl.ds(place, 1), :] == line.astype(F32)
                at = rows_at(n, place)
                sel[r, at] = jnp.where(hit, 1.0, 0.0).astype(BF16)
                gsel[r, at] = jnp.where(hit, slots[1, pl.ds(place, 1), :], 0.0).astype(BF16)

            loop(0, side, body)

    def build_perm():
        for n, (first, count) in enumerate(chunks):
            def body(place):
                shape = (count, side * count)
                line = lax.broadcasted_iota(jnp.int32, shape, 0)
                lane = lax.broadcasted_iota(jnp.int32, shape, 1)
                other = line % side
                source = other * count + (line - other) + place
                perm[rows_at(n, place), :side * count] = jnp.where(source == lane, 1.0, 0.0).astype(BF16)

            loop(0, side, body)

    def permuted(n, ref, start, size):
        first, count = chunks[n]
        matrix = perm[all_rows(n), :side * count]
        return dot(matrix, ref[:, pl.ds(start, size)]).astype(BF16)

    def await_gather(q):
        own_block(q).wait()
        await_ring(side, functools.partial(gather_copy, q))

    def dispatch(q, n):
        r = route_of[q]

        def body(start, size):
            at = pl.ds(start, size)
            sending[q, all_rows(n), at] = dot(sel[r, all_rows(n)], gathered[q, :, at]).astype(BF16)

        column_tiles(ft.shape[1], tile, body)
        start_ring(side, functools.partial(row_copy, q, n))
        here = rows_at(n, m)
        arrived[q, here] = sending[q, here]

    def project(q, n):
        await_ring(side, functools.partial(row_copy, q, n))
        rows = all_rows(n)

        def product(at, size):
            if q == 2:
                return dot(arrived[q, rows], wd[pl.ds(at, size), :], NT)
            return dot(arrived[q, rows], wu[:, pl.ds(at, size)])

        def theirs(start, size):
            at = pl.multiple_of((1 - c) * half + start, 128)
            pair_tmp[rows, pl.ds(start, size)] = product(at, size).astype(BF16)
            pair_out[q, rows, pl.ds(start, size)] = permuted(n, pair_tmp.at[rows], start, size)

        def ours(start, size):
            at = pl.multiple_of(c * half + start, 128)
            kept[q, rows, pl.ds(start, size)] = product(at, size)

        column_tiles(half, tile, theirs)
        pair_copy(q, n).start()
        column_tiles(half, tile, ours)

    def scatter(q, n):
        pair_copy(q, n).wait_recv()
        rows = all_rows(n)
        xsend[q, rows] = (kept[q, rows] + pair_in[q, rows].astype(F32)).astype(BF16)
        start_ring(nx, functools.partial(scatter_copy, q, n))

    def summed(q, n):
        await_ring(nx, functools.partial(scatter_copy, q, n))
        total = xsend[q, share(n, x)].astype(F32)
        for k in range(1, nx):
            total = total + xrecv[q, share(n, around(x, k, nx))].astype(F32)
        return total

    def activate(r, n):
        if r == 0:
            pre = summed(0, n)
            value = pre / (1.0 + jnp.exp(-pre))
        else:
            pre = summed(1, n)
            grad = summed(2, n)
            sigma = 1.0 / (1.0 + jnp.exp(-pre))
            value = grad * sigma * (1.0 + pre * (1.0 - sigma))
        act[r, c, share(n, x)] = value.astype(BF16)
        start_ring(nx, functools.partial(spread_copy, r, n))

    def share_act(r, n):
        await_ring(nx, functools.partial(spread_copy, r, n))
        pair_act_copy(r, n).start()

    def expand(r, n):
        rows = all_rows(n)

        def product(left, start, at, size):
            if r == 0:
                return dot(left, wd[pl.ds(start, half), pl.ds(at, size)])
            return dot(left, wu[pl.ds(at, size), pl.ds(start, half)], NT)

        def ours(at, size):
            start = pl.multiple_of(c * half, 128)
            res_acc[rows, pl.ds(at, size)] = product(act[r, c, rows], start, at, size)

        column_tiles(ft.shape[1], tile, ours)
        pair_act_copy(r, n).wait_recv()

        def reorder(start, size):
            pair_tmp[rows, pl.ds(start, size)] = permuted(n, act.at[r, 1 - c, rows], start, size)

        column_tiles(half, tile, reorder)

        def theirs(at, size):
            start = pl.multiple_of((1 - c) * half, 128)
            here = pl.ds(at, size)
            total = res_acc[rows, here] + product(pair_tmp[rows], start, at, size)
            res[r, rows, here] = total.astype(BF16)

        column_tiles(ft.shape[1], tile, theirs)
        start_ring(side, functools.partial(return_copy, r, n))
        here = rows_at(n, m)
        returned[r, here] = res[r, here]

    def combine(r):
        for n in range(len(chunks)):
            await_ring(side, functools.partial(return_copy, r, n))

        def body(at, size):
            here = pl.ds(at, size)
            total = dot(gsel[r], returned[r, :, here], TN)
            partial[:, here] = total
            part_send[r, :, here] = total.astype(BF16)

        column_tiles(ft.shape[1], tile, body)
        start_ring(side, functools.partial(reduce_copy, r))
        part_recv_own = pl.ds(j * tok, tok)
        own[r] = partial[part_recv_own]

    def finish(r, out):
        await_ring(side, functools.partial(reduce_copy, r))
        total = own[r]
        for k in range(1, side):
            there = pl.ds(around(j, k, side) * tok, tok)
            total = total + part_recv[r, there].astype(F32)
        out[...] = total.astype(BF16)

    own = {}

    count = len(chunks)
    start_gather(0)
    route_info()
    for r in range(2):
        start_ring(side, functools.partial(info_copy, r))
    build_perm()
    build_select(0)
    await_gather(0)
    start_gather(1)
    for n in range(count):
        dispatch(0, n)
    build_select(1)
    await_gather(1)
    start_gather(2)
    for n in range(count):
        dispatch(1, n)
    load_up.wait()
    load_down.wait()
    for n in range(count):
        project(0, n)
    for n in range(count):
        scatter(0, n)
    await_gather(2)
    for n in range(count):
        dispatch(2, n)
    for n in range(count):
        activate(0, n)
    for n in range(count):
        project(1, n)
    for n in range(count):
        share_act(0, n)
    for n in range(count):
        scatter(1, n)
    for n in range(count):
        expand(0, n)
    for n in range(count):
        project(2, n)
    for n in range(count):
        scatter(2, n)
    for n in range(count):
        activate(1, n)
    combine(0)
    for n in range(count):
        share_act(1, n)
    for n in range(count):
        expand(1, n)
    finish(0, fwd_out)
    combine(1)
    finish(1, grad_out)

    for q in range(3):
        drain_ring(side, functools.partial(gather_copy, q))
        for n in range(count):
            drain_ring(side, functools.partial(row_copy, q, n))
            pair_copy(q, n).wait_send()
            drain_ring(nx, functools.partial(scatter_copy, q, n))
    for r in range(2):
        drain_ring(side, functools.partial(info_copy, r))
        drain_ring(side, functools.partial(reduce_copy, r))
        for n in range(count):
            drain_ring(nx, functools.partial(spread_copy, r, n))
            pair_act_copy(r, n).wait_send()
            drain_ring(side, functools.partial(return_copy, r, n))


def build(mesh, capacity, chunks, tile=256):
    n_pipe, n_expert = mesh.shape["pipe"], mesh.shape["expert"]
    side, nx = math.isqrt(n_expert), n_pipe // 2

    def local(ft, fi, fg, bt, bi, bg, bc, w_up, w_down):
        tok, width = ft.shape
        ff = w_up.shape[2]
        half = ff // 2
        rows = n_expert * capacity
        count = len(chunks)
        ring = side * tok
        dma = pltpu.SemaphoreType.DMA
        vmem = pltpu.VMEM
        widest = side * max(size for _, size in chunks)
        scratch = [
            vmem((width, ff), BF16), vmem((ff, width), BF16),
            vmem((2 * tok, 2 * tok), F32), vmem((2 * tok, 2 * tok), F32),
            vmem((2, n_expert, 2 * tok), F32), vmem((2, n_expert, 2 * tok), F32),
            vmem((2, side, ring), F32),
            vmem((2, rows, ring), BF16), vmem((2, rows, ring), BF16), vmem((rows, widest), BF16),
            vmem((3, ring, width), BF16), vmem((3, rows, width), BF16), vmem((3, rows, width), BF16),
            vmem((3, rows, half), F32), vmem((rows, half), BF16),
            vmem((3, rows, half), BF16), vmem((3, rows, half), BF16),
            vmem((3, rows, half), BF16), vmem((3, rows, half), BF16),
            vmem((2, 2, rows, half), BF16),
            vmem((rows, width), F32), vmem((2, rows, width), BF16), vmem((2, rows, width), BF16),
            vmem((ring, width), F32), vmem((2, ring, width), BF16), vmem((2, ring, width), BF16),
            dma((5,)), dma((2, side)), dma((2, side)), dma((3, side)), dma((3, side)),
            dma((3, count, side)), dma((3, count, side)), dma((3, count)), dma((3, count)),
            dma((3, count, nx)), dma((3, count, nx)), dma((2, count, nx)), dma((2, count, nx)),
            dma((2, count)), dma((2, count)), dma((2, count, side)), dma((2, count, side)),
            dma((2, side)), dma((2, side)),
        ]
        any_spec = pl.BlockSpec(memory_space=pl.ANY)
        vmem_spec = pl.BlockSpec(memory_space=pltpu.VMEM)
        out = jax.ShapeDtypeStruct((tok, width), BF16)
        return pl.pallas_call(
            functools.partial(kernel, side, nx, chunks, tile),
            out_shape=(out, out),
            in_specs=[any_spec, vmem_spec, vmem_spec, any_spec, vmem_spec, vmem_spec, any_spec, any_spec, any_spec],
            out_specs=(vmem_spec, vmem_spec),
            scratch_shapes=scratch,
            compiler_params=pltpu.CompilerParams(
                collective_id=0, has_side_effects=True, vmem_limit_bytes=60 * 2**20
            ),
            cost_estimate=pl.CostEstimate(flops=12 * rows * width * ff, bytes_accessed=6 * width * ff, transcendentals=0),
        )(ft, fi, fg, bt, bi, bg, bc, w_up[0], w_down[0])

    in_specs = (
        P("expert", "pipe"), P("expert", None), P("expert", None),
        P("expert", "pipe"), P("expert", None), P("expert", None),
        P("expert", "pipe"), P("expert", "pipe", None), P("expert", None, "pipe"),
    )
    out_specs = (P("expert", "pipe"), P("expert", "pipe"))
    return jax.shard_map(local, mesh=mesh, in_specs=in_specs, out_specs=out_specs, check_vma=False)


def solution(mesh):
    return build(mesh, 10, ((0, 48), (48, 32)))
```

time: 411 us -> 169 us (0.41)
  the two profiles are of different devices: /device:TPU:6 before, /device:TPU:1 now
where the time goes in v1:
time: 169 us
  Pallas kernels  160 us (95%)
  local copies, waits for them, and re-layouts  8.63 us (5%)
    pallas_call x1, Pallas kernels, local(): pl.pallas_call(functools.partial(kernel, side, nx, chunks, tile), out_sha...  160 us
    unnamed x6, local copies, waits for them, and re-layouts  8.63 us

profile of v1, /device:TPU:1, one launch (start us, length us, event | category | flops | bytes accessed | tf_op | source)
XLA Modules:
  0.0 169.0 jit_solution(3144621623577730869)
XLA Ops:
  0.6 1.4 copy.11.fi
  2.0 1.4 copy.12.fg
  3.4 1.4 copy.13.bi
  4.8 1.4 copy.14.bg
  6.2 159.7 %shard_map.104 = (bf16[64,896]{1,0:T(8,128)(2,1)}, bf16[64,896]{1,0:T(8,128)(2,1)}) custom-call(bf16[64,896]{1,0:T(8,128)(2,1)} %ft.1, s32[64,8]{1,0:T(8,128)} %copy.11.fi, f32[64,8]{1,0:T(8,128)} %copy.12.fg, bf16[64,896]{1,0:T(8,128)(2,1)} %bt.1, s32[64,8]{1,0:T(8,128)} %copy.13.bi, f32[64,8]{1,0:T(8,128)} %copy.14.bg, bf16[64,896]{1,0:T(8,128)(2,1)} %bc.1, ...), custom_call_target="tpu_custom_call" | custom-call | flops 7046430720 | bytes 5505024 | tf_op jit(solution)/shard_map/pallas_call | solution.py:472
  165.9 1.6 copy.17
  167.4 1.6 copy.18

commit v2 on v1

--- a/solution.py
+++ b/solution.py
@@ -37,13 +37,14 @@
     side, nx, chunks, tile,
     ft, fi, fg, bt, bi, bg, bc, wu_hbm, wd_hbm,
     fwd_out, grad_out,
-    wu, wd, ids, ids_t, info_own, info_all, slots, sel, gsel, perm,
+    wu, wd, ids, gates, info_own, info_all, slots, sel, gsel, perm,
     gathered, sending, arrived, kept, pair_tmp, pair_out, pair_in, xsend, xrecv,
-    act, res_acc, res, returned, partial, part_send, part_recv,
+    act, res_acc, res, returned, partial, part_send, part_recv, fold,
     lsem, info_s, info_r, gat_s, gat_r, a2a_s, a2a_r, pr1_s, pr1_r, xrs_s, xrs_r,
     xag_s, xag_r, pr2_s, pr2_r, ret_s, ret_r, red_s, red_r,
 ):
     tok = ft.shape[0]
+    part = tok // 2
     half = wu.shape[1] // 2
     p = lax.axis_index("pipe")
     e = lax.axis_index("expert")
@@ -91,6 +92,12 @@
     load_down = pltpu.make_async_copy(wd_hbm, wd, lsem.at[4])
     for q in range(3):
         own_block(q).start()
+    small = tuple(
+        pltpu.make_async_copy(ref, into, lsem.at[5 + at])
+        for at, (ref, into) in enumerate(((fi, ids.at[0]), (fg, gates.at[0]), (bi, ids.at[1]), (bg, gates.at[1])))
+    )
+    for copy in small:
+        copy.start()
     load_up.start()
     load_down.start()
 
@@ -103,9 +110,23 @@
     pl.semaphore_signal(barrier, inc=1, device_id=core_dev, device_id_type=MESH)
     pl.semaphore_wait(barrier, 2 * (side - 1) + nx)
 
-    def gather_copy(q, k):
-        here = gathered.at[q, pl.ds(j * tok, tok)]
-        return remote(tokens[q], here, gat_s.at[q, k], gat_r.at[q, k], gather_dev(around(j, k, side)))
+    def block(place):
+        return pl.ds(pl.multiple_of(place * tok, tok), tok)
+
+    GATHER = (
+        (0, 1, None), (0, -1, None), (0, 2, None), (0, -2, None),
+        (-2, 1, None), (2, -1, None), (-2, 2, 0), (2, -2, 1),
+    )
+
+    def gather_copy(q, kind):
+        origin, target, piece = GATHER[kind]
+        place = around(j, side + origin, side)
+        rows = block(place)
+        if piece is not None:
+            rows = pl.ds(pl.multiple_of(place * tok + piece * part, part), part)
+        here = gathered.at[q, rows]
+        source = tokens[q] if origin == 0 else here
+        return remote(source, here, gat_s.at[q, kind], gat_r.at[q, kind], gather_dev(around(j, side + target, side)))
 
     def info_copy(r, k):
         there = around(j, k, side)
@@ -132,12 +153,21 @@
             ret_s.at[r, n, k], ret_r.at[r, n, k], row_dev(there),
         )
 
-    def reduce_copy(r, k):
-        there = around(j, k, side)
-        return remote(
-            part_send.at[r, pl.ds(there * tok, tok)], part_recv.at[r, pl.ds(j * tok, tok)],
-            red_s.at[r, k], red_r.at[r, k], gather_dev(there),
-        )
+    REDUCE = (
+        (1, 1, None), (-1, -1, None), (3, 1, None), (-3, -1, None),
+        (4, 2, 1), (4, -2, 0), (2, 2, None), (-2, -2, None),
+    )
+
+    def reduce_copy(r, kind):
+        owner, target, piece = REDUCE[kind]
+        place = around(j, side + owner, side)
+        source, there = part_send.at[r, block(place)], part_recv.at[r, kind]
+        if kind >= 6:
+            source = fold.at[r, kind - 6]
+        if piece is not None:
+            source = part_send.at[r, pl.ds(pl.multiple_of(place * tok + piece * part, part), part)]
+            there = part_recv.at[r, kind, pl.ds(piece * part, part)]
+        return remote(source, there, red_s.at[r, kind], red_r.at[r, kind], gather_dev(around(j, side + target, side)))
 
     def all_rows(n):
         first, count = chunks[n]
@@ -179,38 +209,41 @@
         loop(1, size, lambda k: copy(k).wait_send())
 
     def start_gather(q):
-        start_ring(side, functools.partial(gather_copy, q))
+        for kind in (2, 3, 0, 1):
+            gather_copy(q, kind).start()
+
+    def pass_on(q):
+        for kind in (2, 3):
+            gather_copy(q, kind).wait_recv()
+            gather_copy(q, kind + 4).start()
+            gather_copy(q, kind + 2).start()
 
     def route_info():
-        rows = ids.shape[0]
-        ids[...] = jnp.zeros_like(ids)
-        for at in (0, rows // 2):
-            for place, ref in enumerate((fi, fg, bi, bg)):
-                width = ref.shape[1]
-                ids[at:at + tok, place * width:(place + 1) * width] = ref[...].astype(F32)
-        ids_t[...] = ids[...].T
-        top = fi.shape[1]
+        for copy in small:
+            copy.wait()
         shape = (side * side, 2 * tok)
         row = lax.broadcasted_iota(jnp.int32, shape, 0)
         lane = lax.broadcasted_iota(jnp.int32, shape, 1)
-        expert = ((row // side) * sj + (row % side) * sm).astype(F32)
+        expert = (row // side) * sj + (row % side) * sm
         wide = (2 * tok, 2 * tok)
         before = lax.broadcasted_iota(jnp.int32, wide, 0)
         after = lax.broadcasted_iota(jnp.int32, wide, 1)
         earlier = jnp.where((before < after) & (after < tok), 1.0, 0.0).astype(BF16)
         for r in range(2):
+            names = jnp.concatenate([ids[r], ids[r]], axis=1)
+            weights = jnp.concatenate([gates[r], gates[r]], axis=1)
             named = jnp.zeros(shape, F32)
             gate = jnp.zeros(shape, F32)
-            for k in range(top):
-                at = 2 * top * r + k
-                hit = ids_t[at:at + 1, :] == expert
+            for k in range(ids.shape[1]):
+                hit = names[k:k + 1, :] == expert
                 named = named + jnp.where(hit, 1.0, 0.0)
-                gate = gate + jnp.where(hit, ids_t[at + top:at + top + 1, :], 0.0)
+                gate = gate + jnp.where(hit, weights[k:k + 1, :], 0.0)
             rank = dot(named.astype(BF16), earlier)
             slot = jnp.where(named > 0.5, rank * side + j.astype(F32), -1.0)
             info_own[r] = jnp.where(lane < tok, slot, gate)
-            here = pl.ds(j * side, side)
+            here = pl.ds(pl.multiple_of(j * side, side), side)
             info_all[r, here] = info_own[r, here]
+            start_ring(side, functools.partial(info_copy, r))
 
     def build_select(r):
         await_ring(side, functools.partial(info_copy, r))
@@ -247,7 +280,8 @@
 
     def await_gather(q):
         own_block(q).wait()
-        await_ring(side, functools.partial(gather_copy, q))
+        for kind in (0, 1, 4, 5, 6, 7):
+            gather_copy(q, kind).wait_recv()
 
     def dispatch(q, n):
         r = route_of[q]
@@ -343,91 +377,110 @@
         here = rows_at(n, m)
         returned[r, here] = res[r, here]
 
-    def combine(r):
-        for n in range(len(chunks)):
-            await_ring(side, functools.partial(return_copy, r, n))
+    def combine(r, n):
+        await_ring(side, functools.partial(return_copy, r, n))
+        rows = all_rows(n)
+        last = n == len(chunks) - 1
 
         def body(at, size):
             here = pl.ds(at, size)
-            total = dot(gsel[r], returned[r, :, here], TN)
-            partial[:, here] = total
-            part_send[r, :, here] = total.astype(BF16)
+            total = dot(gsel[r, rows], returned[r, rows, here], TN)
+            if n:
+                total = total + partial[r, :, here]
+            partial[r, :, here] = total
+            if last:
+                part_send[r, :, here] = total.astype(BF16)
 
         column_tiles(ft.shape[1], tile, body)
-        start_ring(side, functools.partial(reduce_copy, r))
-        part_recv_own = pl.ds(j * tok, tok)
-        own[r] = partial[part_recv_own]
+        if last:
+            for kind in (4, 5, 2, 3, 0, 1):
+                reduce_copy(r, kind).start()
+
+    def fold_in(r):
+        for kind in (2, 3, 4, 5):
+            reduce_copy(r, kind).wait_recv()
+        for at, owner in enumerate((2, -2)):
+            mine = block(around(j, side + owner, side))
+            fold[r, at] = (partial[r, mine] + part_recv[r, 2 + at].astype(F32)).astype(BF16)
+            piece = pl.ds((1 - at) * part, part)
+            extra = pl.ds(pl.multiple_of(around(j, side + owner, side) * tok + (1 - at) * part, part), part)
+            total = partial[r, extra] + part_recv[r, 2 + at, piece].astype(F32)
+            fold[r, at, piece] = (total + part_recv[r, 4 + at, piece].astype(F32)).astype(BF16)
+            reduce_copy(r, 6 + at).start()
 
     def finish(r, out):
-        await_ring(side, functools.partial(reduce_copy, r))
-        total = own[r]
-        for k in range(1, side):
-            there = pl.ds(around(j, k, side) * tok, tok)
-            total = total + part_recv[r, there].astype(F32)
+        total = partial[r, block(j)]
+        for kind in (0, 1, 6, 7):
+            reduce_copy(r, kind).wait_recv()
+            total = total + part_recv[r, kind].astype(F32)
         out[...] = total.astype(BF16)
 
-    own = {}
-
-    count = len(chunks)
     start_gather(0)
+    start_gather(1)
+    start_gather(2)
     route_info()
-    for r in range(2):
-        start_ring(side, functools.partial(info_copy, r))
     build_perm()
+    pass_on(0)
+    pass_on(1)
     build_select(0)
+    pass_on(2)
+    build_select(1)
     await_gather(0)
-    start_gather(1)
-    for n in range(count):
-        dispatch(0, n)
-    build_select(1)
+    dispatch(0, 0)
     await_gather(1)
-    start_gather(2)
-    for n in range(count):
-        dispatch(1, n)
+    dispatch(0, 1)
+    dispatch(1, 0)
+    await_gather(2)
+    dispatch(2, 0)
     load_up.wait()
     load_down.wait()
-    for n in range(count):
-        project(0, n)
-    for n in range(count):
-        scatter(0, n)
-    await_gather(2)
-    for n in range(count):
-        dispatch(2, n)
-    for n in range(count):
-        activate(0, n)
-    for n in range(count):
-        project(1, n)
-    for n in range(count):
-        share_act(0, n)
-    for n in range(count):
-        scatter(1, n)
-    for n in range(count):
-        expand(0, n)
-    for n in range(count):
-        project(2, n)
-    for n in range(count):
-        scatter(2, n)
-    for n in range(count):
-        activate(1, n)
-    combine(0)
-    for n in range(count):
-        share_act(1, n)
-    for n in range(count):
-        expand(1, n)
+    project(0, 0)
+    scatter(0, 0)
+    dispatch(1, 1)
+    project(0, 1)
+    scatter(0, 1)
+    dispatch(2, 1)
+    activate(0, 0)
+    activate(0, 1)
+    project(1, 0)
+    scatter(1, 0)
+    share_act(0, 0)
+    share_act(0, 1)
+    expand(0, 0)
+    expand(0, 1)
+    project(2, 0)
+    scatter(2, 0)
+    project(1, 1)
+    scatter(1, 1)
+    activate(1, 0)
+    project(2, 1)
+    scatter(2, 1)
+    combine(0, 0)
+    combine(0, 1)
+    share_act(1, 0)
+    expand(1, 0)
+    activate(1, 1)
+    share_act(1, 1)
+    expand(1, 1)
+    fold_in(0)
+    combine(1, 0)
+    combine(1, 1)
     finish(0, fwd_out)
-    combine(1)
+    fold_in(1)
     finish(1, grad_out)
 
     for q in range(3):
-        drain_ring(side, functools.partial(gather_copy, q))
-        for n in range(count):
+        for kind in range(8):
+            gather_copy(q, kind).wait_send()
+        for n in range(len(chunks)):
             drain_ring(side, functools.partial(row_copy, q, n))
             pair_copy(q, n).wait_send()
             drain_ring(nx, functools.partial(scatter_copy, q, n))
     for r in range(2):
         drain_ring(side, functools.partial(info_copy, r))
-        drain_ring(side, functools.partial(reduce_copy, r))
-        for n in range(count):
+        for kind in range(8):
+            reduce_copy(r, kind).wait_send()
+        for n in range(len(chunks)):
             drain_ring(nx, functools.partial(spread_copy, r, n))
             pair_act_copy(r, n).wait_send()
             drain_ring(side, functools.partial(return_copy, r, n))
@@ -439,6 +492,7 @@
 
     def local(ft, fi, fg, bt, bi, bg, bc, w_up, w_down):
         tok, width = ft.shape
+        top = fi.shape[1]
         ff = w_up.shape[2]
         half = ff // 2
         rows = n_expert * capacity
@@ -449,7 +503,7 @@
         widest = side * max(size for _, size in chunks)
         scratch = [
             vmem((width, ff), BF16), vmem((ff, width), BF16),
-            vmem((2 * tok, 2 * tok), F32), vmem((2 * tok, 2 * tok), F32),
+            vmem((2, top, tok), jnp.int32), vmem((2, top, tok), F32),
             vmem((2, n_expert, 2 * tok), F32), vmem((2, n_expert, 2 * tok), F32),
             vmem((2, side, ring), F32),
             vmem((2, rows, ring), BF16), vmem((2, rows, ring), BF16), vmem((rows, widest), BF16),
@@ -459,12 +513,13 @@
             vmem((3, rows, half), BF16), vmem((3, rows, half), BF16),
             vmem((2, 2, rows, half), BF16),
             vmem((rows, width), F32), vmem((2, rows, width), BF16), vmem((2, rows, width), BF16),
-            vmem((ring, width), F32), vmem((2, ring, width), BF16), vmem((2, ring, width), BF16),
-            dma((5,)), dma((2, side)), dma((2, side)), dma((3, side)), dma((3, side)),
+            vmem((2, ring, width), F32), vmem((2, ring, width), BF16), vmem((2, 8, tok, width), BF16),
+            vmem((2, 2, tok, width), BF16),
+            dma((9,)), dma((2, side)), dma((2, side)), dma((3, 8)), dma((3, 8)),
             dma((3, count, side)), dma((3, count, side)), dma((3, count)), dma((3, count)),
             dma((3, count, nx)), dma((3, count, nx)), dma((2, count, nx)), dma((2, count, nx)),
             dma((2, count)), dma((2, count)), dma((2, count, side)), dma((2, count, side)),
-            dma((2, side)), dma((2, side)),
+            dma((2, 8)), dma((2, 8)),
         ]
         any_spec = pl.BlockSpec(memory_space=pl.ANY)
         vmem_spec = pl.BlockSpec(memory_space=pltpu.VMEM)
@@ -472,14 +527,14 @@
         return pl.pallas_call(
             functools.partial(kernel, side, nx, chunks, tile),
             out_shape=(out, out),
-            in_specs=[any_spec, vmem_spec, vmem_spec, any_spec, vmem_spec, vmem_spec, any_spec, any_spec, any_spec],
+            in_specs=[any_spec] * 9,
             out_specs=(vmem_spec, vmem_spec),
             scratch_shapes=scratch,
             compiler_params=pltpu.CompilerParams(
                 collective_id=0, has_side_effects=True, vmem_limit_bytes=60 * 2**20
             ),
             cost_estimate=pl.CostEstimate(flops=12 * rows * width * ff, bytes_accessed=6 * width * ff, transcendentals=0),
-        )(ft, fi, fg, bt, bi, bg, bc, w_up[0], w_down[0])
+        )(ft, fi.T, fg.T, bt, bi.T, bg.T, bc, w_up[0], w_down[0])
 
     in_specs = (
         P("expert", "pipe"), P("expert", None), P("expert", None),

time: 169 us -> 132 us (0.78)
  the two profiles are of different devices: /device:TPU:1 before, /device:TPU:6 now
where the time goes in v2:
time: 132 us; the launch traced here: 131 us
  Pallas kernels  128 us (97%)
  local copies, waits for them, and re-layouts  3.11 us (2%)
    pallas_call x1, Pallas kernels, local(): pl.pallas_call(functools.partial(kernel, side, nx, chunks, tile), out_sha...  128 us
    unnamed x2, local copies, waits for them, and re-layouts  3.11 us

profile of v2, /device:TPU:6, one launch (start us, length us, event | category | flops | bytes accessed | tf_op | source)
XLA Modules:
  0.0 131.3 jit_solution(1449137471153972704)
XLA Ops:
  0.6 127.6 %shard_map.104 = (bf16[64,896]{1,0:T(8,128)(2,1)}, bf16[64,896]{1,0:T(8,128)(2,1)}) custom-call(bf16[64,896]{1,0:T(8,128)(2,1)} %ft.1, s32[8,64]{1,0:T(8,128)} %bitcast.8, f32[8,64]{1,0:T(8,128)} %bitcast.9, bf16[64,896]{1,0:T(8,128)(2,1)} %bt.1, s32[8,64]{1,0:T(8,128)} %bitcast.10, f32[8,64]{1,0:T(8,128)} %bitcast.11, bf16[64,896]{1,0:T(8,128)(2,1)} %bc.1, ...), custom_call_target="tpu_custom_call" | custom-call | flops 7046430720 | bytes 5505024 | tf_op jit(solution)/shard_map/pallas_call | solution.py:527
  128.2 1.6 %copy.13 = bf16[64,896]{1,0:T(8,128)(2,1)} copy(bf16[64,896]{1,0:T(8,128)(2,1)} %get-tuple-element.4) | data formatting | bytes 229376
  129.8 1.6 %copy.14 = bf16[64,896]{1,0:T(8,128)(2,1)} copy(bf16[64,896]{1,0:T(8,128)(2,1)} %get-tuple-element.5) | data formatting | bytes 229376

commit v3 on v2

--- a/solution.py
+++ b/solution.py
@@ -36,10 +36,10 @@
 def kernel(
     side, nx, chunks, tile,
     ft, fi, fg, bt, bi, bg, bc, wu_hbm, wd_hbm,
-    fwd_out, grad_out,
+    both_out,
     wu, wd, ids, gates, info_own, info_all, slots, sel, gsel, perm,
     gathered, sending, arrived, kept, pair_tmp, pair_out, pair_in, xsend, xrecv,
-    act, res_acc, res, returned, partial, part_send, part_recv, fold,
+    act, res_acc, res, returned, partial, part_send, part_recv, fold, result,
     lsem, info_s, info_r, gat_s, gat_r, a2a_s, a2a_r, pr1_s, pr1_r, xrs_s, xrs_r,
     xag_s, xag_r, pr2_s, pr2_r, ret_s, ret_r, red_s, red_r,
 ):
@@ -114,7 +114,7 @@
         return pl.ds(pl.multiple_of(place * tok, tok), tok)
 
     GATHER = (
-        (0, 1, None), (0, -1, None), (0, 2, None), (0, -2, None),
+        (0, 1, None), (0, -1, None), (-1, 1, None), (1, -1, None),
         (-2, 1, None), (2, -1, None), (-2, 2, 0), (2, -2, 1),
     )
 
@@ -132,8 +132,12 @@
         there = around(j, k, side)
         return remote(
             info_own.at[r, pl.ds(there * side, side)], info_all.at[r, pl.ds(j * side, side)],
-            info_s.at[r, k], info_r.at[r, k], gather_dev(there),
-        )
+            info_s.at[r], info_r.at[r], gather_dev(there),
+        )
+
+    def info_copies(r):
+        rows = pl.ds(0, (side - 1) * side)
+        return remote(info_own.at[r, rows], info_all.at[r, rows], info_s.at[r], info_r.at[r], gather_dev(around(j, 1, side)))
 
     def rows_at(n, place):
         first, count = chunks[n]
@@ -143,14 +147,41 @@
         there = around(m, k, side)
         return remote(
             sending.at[q, rows_at(n, there)], arrived.at[q, rows_at(n, m)],
-            a2a_s.at[q, n, k], a2a_r.at[q, n, k], row_dev(there),
-        )
-
-    def return_copy(r, n, k):
+            a2a_s.at[q, n], a2a_r.at[q, n], row_dev(there),
+        )
+
+    def most_rows(n):
+        first, count = chunks[n]
+        return pl.ds(side * first, (side - 1) * count)
+
+    def row_copies(q, n):
+        rows = most_rows(n)
+        return remote(
+            sending.at[q, rows], arrived.at[q, rows], a2a_s.at[q, n], a2a_r.at[q, n], row_dev(around(m, 1, side)),
+        )
+
+    width = ft.shape[1]
+    last = len(chunks) - 1
+
+    def reduce_spans(r):
+        return ((0, half), (half, width - half)) if r else ((0, width),)
+
+    def return_spans(r, n):
+        return reduce_spans(r) if n == last else ((0, width),)
+
+    def return_copy(r, n, h, k):
         there = around(m, k, side)
-        return remote(
-            res.at[r, rows_at(n, there)], returned.at[r, rows_at(n, m)],
-            ret_s.at[r, n, k], ret_r.at[r, n, k], row_dev(there),
+        at = pl.ds(*return_spans(r, n)[h])
+        return remote(
+            res.at[r, rows_at(n, there), at], returned.at[r, rows_at(n, m), at],
+            ret_s.at[r, n, h], ret_r.at[r, n, h], row_dev(there),
+        )
+
+    def return_copies(r, n, h):
+        rows, at = most_rows(n), pl.ds(*return_spans(r, n)[h])
+        return remote(
+            res.at[r, rows, at], returned.at[r, rows, at],
+            ret_s.at[r, n, h], ret_r.at[r, n, h], row_dev(around(m, 1, side)),
         )
 
     REDUCE = (
@@ -158,16 +189,22 @@
         (4, 2, 1), (4, -2, 0), (2, 2, None), (-2, -2, None),
     )
 
-    def reduce_copy(r, kind):
+    def reduce_copy(r, h, kind):
         owner, target, piece = REDUCE[kind]
         place = around(j, side + owner, side)
-        source, there = part_send.at[r, block(place)], part_recv.at[r, kind]
+        at = pl.ds(*reduce_spans(r)[h])
+        source, there = part_send.at[r, block(place), at], part_recv.at[r, kind, :, at]
         if kind >= 6:
-            source = fold.at[r, kind - 6]
+            source = fold.at[r, kind - 6, :, at]
         if piece is not None:
-            source = part_send.at[r, pl.ds(pl.multiple_of(place * tok + piece * part, part), part)]
-            there = part_recv.at[r, kind, pl.ds(piece * part, part)]
-        return remote(source, there, red_s.at[r, kind], red_r.at[r, kind], gather_dev(around(j, side + target, side)))
+            source = part_send.at[r, pl.ds(pl.multiple_of(place * tok + piece * part, part), part), at]
+            there = part_recv.at[r, kind, pl.ds(piece * part, part), at]
+        device = gather_dev(around(j, side + target, side))
+        return remote(source, there, red_s.at[r, h, kind], red_r.at[r, h, kind], device)
+
+    def out_copy(r, h):
+        at = pl.ds(*reduce_spans(r)[h])
+        return pltpu.make_async_copy(result.at[r, :, at], both_out.at[r, :, at], lsem.at[9 + r + h])
 
     def all_rows(n):
         first, count = chunks[n]
@@ -188,12 +225,26 @@
         there = around(x, k, nx)
         return remote(
             xsend.at[q, share(n, there)], xrecv.at[q, share(n, x)],
-            xrs_s.at[q, n, k], xrs_r.at[q, n, k], x_dev(there),
+            xrs_s.at[q, n], xrs_r.at[q, n], x_dev(there),
+        )
+
+    def other_shares(n):
+        first, count = chunks[n]
+        return pl.ds(side * first, (nx - 1) * (side * count // nx))
+
+    def scatter_copies(q, n):
+        rows = other_shares(n)
+        return remote(
+            xsend.at[q, rows], xrecv.at[q, rows], xrs_s.at[q, n], xrs_r.at[q, n], x_dev(around(x, 1, nx)),
         )
 
     def spread_copy(r, n, k):
         here = act.at[r, c, share(n, x)]
-        return remote(here, here, xag_s.at[r, n, k], xag_r.at[r, n, k], x_dev(around(x, k, nx)))
+        return remote(here, here, xag_s.at[r, n], xag_r.at[r, n], x_dev(around(x, k, nx)))
+
+    def spread_copies(r, n):
+        here = act.at[r, c, other_shares(n)]
+        return remote(here, here, xag_s.at[r, n], xag_r.at[r, n], x_dev(around(x, 1, nx)))
 
     def pair_act_copy(r, n):
         here = act.at[r, c, all_rows(n)]
@@ -202,15 +253,14 @@
     def start_ring(size, copy):
         loop(1, size, lambda k: copy(k).start())
 
-    def await_ring(size, copy):
-        loop(1, size, lambda k: copy(k).wait_recv())
-
-    def drain_ring(size, copy):
-        loop(1, size, lambda k: copy(k).wait_send())
-
     def start_gather(q):
-        for kind in (2, 3, 0, 1):
+        for kind in (0, 1):
             gather_copy(q, kind).start()
+
+    def pass_first(q):
+        for kind in (0, 1):
+            gather_copy(q, kind).wait_recv()
+            gather_copy(q, kind + 2).start()
 
     def pass_on(q):
         for kind in (2, 3):
@@ -246,7 +296,7 @@
             start_ring(side, functools.partial(info_copy, r))
 
     def build_select(r):
-        await_ring(side, functools.partial(info_copy, r))
+        info_copies(r).wait_recv()
         for b in range(side):
             here = info_all[r, b * side:(b + 1) * side, :]
             slots[0, :, b * tok:(b + 1) * tok] = here[:, :tok]
@@ -280,7 +330,7 @@
 
     def await_gather(q):
         own_block(q).wait()
-        for kind in (0, 1, 4, 5, 6, 7):
+        for kind in (4, 5, 6, 7):
             gather_copy(q, kind).wait_recv()
 
     def dispatch(q, n):
@@ -290,13 +340,13 @@
             at = pl.ds(start, size)
             sending[q, all_rows(n), at] = dot(sel[r, all_rows(n)], gathered[q, :, at]).astype(BF16)
 
-        column_tiles(ft.shape[1], tile, body)
+        column_tiles(width, tile, body)
         start_ring(side, functools.partial(row_copy, q, n))
         here = rows_at(n, m)
         arrived[q, here] = sending[q, here]
 
     def project(q, n):
-        await_ring(side, functools.partial(row_copy, q, n))
+        row_copies(q, n).wait_recv()
         rows = all_rows(n)
 
         def product(at, size):
@@ -324,7 +374,7 @@
         start_ring(nx, functools.partial(scatter_copy, q, n))
 
     def summed(q, n):
-        await_ring(nx, functools.partial(scatter_copy, q, n))
+        scatter_copies(q, n).wait_recv()
         total = xsend[q, share(n, x)].astype(F32)
         for k in range(1, nx):
             total = total + xrecv[q, share(n, around(x, k, nx))].astype(F32)
@@ -343,7 +393,7 @@
         start_ring(nx, functools.partial(spread_copy, r, n))
 
     def share_act(r, n):
-        await_ring(nx, functools.partial(spread_copy, r, n))
+        spread_copies(r, n).wait_recv()
         pair_act_copy(r, n).start()
 
     def expand(r, n):
@@ -358,7 +408,7 @@
             start = pl.multiple_of(c * half, 128)
             res_acc[rows, pl.ds(at, size)] = product(act[r, c, rows], start, at, size)
 
-        column_tiles(ft.shape[1], tile, ours)
+        column_tiles(width, tile, ours)
         pair_act_copy(r, n).wait_recv()
 
         def reorder(start, size):
@@ -372,63 +422,89 @@
             total = res_acc[rows, here] + product(pair_tmp[rows], start, at, size)
             res[r, rows, here] = total.astype(BF16)
 
-        column_tiles(ft.shape[1], tile, theirs)
-        start_ring(side, functools.partial(return_copy, r, n))
+        for h, (at, size) in enumerate(return_spans(r, n)):
+            column_tiles(size, tile, lambda start, count, at=at: theirs(at + start, count))
+            start_ring(side, functools.partial(return_copy, r, n, h))
         here = rows_at(n, m)
         returned[r, here] = res[r, here]
 
-    def combine(r, n):
-        await_ring(side, functools.partial(return_copy, r, n))
+    def combine(r, n, h):
+        if n == last or h == 0:
+            return_copies(r, n, h).wait_recv()
         rows = all_rows(n)
-        last = n == len(chunks) - 1
+        base, columns = reduce_spans(r)[h]
 
         def body(at, size):
-            here = pl.ds(at, size)
+            here = pl.ds(base + at, size)
             total = dot(gsel[r, rows], returned[r, rows, here], TN)
             if n:
                 total = total + partial[r, :, here]
             partial[r, :, here] = total
-            if last:
+            if n == last:
                 part_send[r, :, here] = total.astype(BF16)
 
-        column_tiles(ft.shape[1], tile, body)
-        if last:
+        column_tiles(columns, tile, body)
+        if n == last:
             for kind in (4, 5, 2, 3, 0, 1):
-                reduce_copy(r, kind).start()
-
-    def fold_in(r):
+                reduce_copy(r, h, kind).start()
+
+    def fold_in(r, h):
         for kind in (2, 3, 4, 5):
-            reduce_copy(r, kind).wait_recv()
-        for at, owner in enumerate((2, -2)):
-            mine = block(around(j, side + owner, side))
-            fold[r, at] = (partial[r, mine] + part_recv[r, 2 + at].astype(F32)).astype(BF16)
-            piece = pl.ds((1 - at) * part, part)
-            extra = pl.ds(pl.multiple_of(around(j, side + owner, side) * tok + (1 - at) * part, part), part)
-            total = partial[r, extra] + part_recv[r, 2 + at, piece].astype(F32)
-            fold[r, at, piece] = (total + part_recv[r, 4 + at, piece].astype(F32)).astype(BF16)
-            reduce_copy(r, 6 + at).start()
-
-    def finish(r, out):
-        total = partial[r, block(j)]
+            reduce_copy(r, h, kind).wait_recv()
+        at = pl.ds(*reduce_spans(r)[h])
+        for place, owner in enumerate((2, -2)):
+            start = around(j, side + owner, side) * tok
+            for piece in range(2):
+                mine = pl.ds(pl.multiple_of(start + piece * part, part), part)
+                here = pl.ds(piece * part, part)
+                total = partial[r, mine, at] + part_recv[r, 2 + place, here, at].astype(F32)
+                if piece == 1 - place:
+                    total = total + part_recv[r, 4 + place, here, at].astype(F32)
+                fold[r, place, here, at] = total.astype(BF16)
+            reduce_copy(r, h, 6 + place).start()
+
+    def finish(r, h):
+        at = pl.ds(*reduce_spans(r)[h])
+        total = partial[r, block(j), at]
         for kind in (0, 1, 6, 7):
-            reduce_copy(r, kind).wait_recv()
-            total = total + part_recv[r, kind].astype(F32)
-        out[...] = total.astype(BF16)
+            reduce_copy(r, h, kind).wait_recv()
+            total = total + part_recv[r, kind, :, at].astype(F32)
+        result[r, :, at] = total.astype(BF16)
+        out_copy(r, h).start()
+
+    def drain():
+        for q in range(3):
+            for kind in range(8):
+                gather_copy(q, kind).wait_send()
+            for n in range(len(chunks)):
+                row_copies(q, n).wait_send()
+                pair_copy(q, n).wait_send()
+                scatter_copies(q, n).wait_send()
+        for r in range(2):
+            info_copies(r).wait_send()
+            for n in range(len(chunks)):
+                spread_copies(r, n).wait_send()
+                pair_act_copy(r, n).wait_send()
+                for h in range(len(return_spans(r, n))):
+                    return_copies(r, n, h).wait_send()
 
     start_gather(0)
     start_gather(1)
     start_gather(2)
     route_info()
     build_perm()
+    pass_first(0)
+    pass_first(1)
+    pass_first(2)
+    build_select(0)
     pass_on(0)
     pass_on(1)
-    build_select(0)
     pass_on(2)
     build_select(1)
     await_gather(0)
     dispatch(0, 0)
+    dispatch(0, 1)
     await_gather(1)
-    dispatch(0, 1)
     dispatch(1, 0)
     await_gather(2)
     dispatch(2, 0)
@@ -441,52 +517,47 @@
     scatter(0, 1)
     dispatch(2, 1)
     activate(0, 0)
-    activate(0, 1)
     project(1, 0)
     scatter(1, 0)
+    activate(0, 1)
     share_act(0, 0)
-    share_act(0, 1)
     expand(0, 0)
-    expand(0, 1)
     project(2, 0)
     scatter(2, 0)
+    share_act(0, 1)
+    expand(0, 1)
     project(1, 1)
     scatter(1, 1)
     activate(1, 0)
     project(2, 1)
     scatter(2, 1)
-    combine(0, 0)
-    combine(0, 1)
     share_act(1, 0)
     expand(1, 0)
+    combine(0, 0, 0)
+    combine(0, 1, 0)
     activate(1, 1)
     share_act(1, 1)
     expand(1, 1)
-    fold_in(0)
-    combine(1, 0)
-    combine(1, 1)
-    finish(0, fwd_out)
-    fold_in(1)
-    finish(1, grad_out)
-
-    for q in range(3):
-        for kind in range(8):
-            gather_copy(q, kind).wait_send()
-        for n in range(len(chunks)):
-            drain_ring(side, functools.partial(row_copy, q, n))
-            pair_copy(q, n).wait_send()
-            drain_ring(nx, functools.partial(scatter_copy, q, n))
+    fold_in(0, 0)
+    combine(1, 0, 0)
+    combine(1, 0, 1)
+    combine(1, 1, 0)
+    combine(1, 1, 1)
+    finish(0, 0)
+    fold_in(1, 0)
+    fold_in(1, 1)
+    drain()
+    finish(1, 0)
+    finish(1, 1)
+
     for r in range(2):
-        drain_ring(side, functools.partial(info_copy, r))
-        for kind in range(8):
-            reduce_copy(r, kind).wait_send()
-        for n in range(len(chunks)):
-            drain_ring(nx, functools.partial(spread_copy, r, n))
-            pair_act_copy(r, n).wait_send()
-            drain_ring(side, functools.partial(return_copy, r, n))
-
-
-def build(mesh, capacity, chunks, tile=256):
+        for h in range(len(reduce_spans(r))):
+            for kind in range(8):
+                reduce_copy(r, h, kind).wait_send()
+            out_copy(r, h).wait()
+
+
+def build(mesh, capacity, chunks, tile=512):
     n_pipe, n_expert = mesh.shape["pipe"], mesh.shape["expert"]
     side, nx = math.isqrt(n_expert), n_pipe // 2
 
@@ -514,27 +585,27 @@
             vmem((2, 2, rows, half), BF16),
             vmem((rows, width), F32), vmem((2, rows, width), BF16), vmem((2, rows, width), BF16),
             vmem((2, ring, width), F32), vmem((2, ring, width), BF16), vmem((2, 8, tok, width), BF16),
-            vmem((2, 2, tok, width), BF16),
-            dma((9,)), dma((2, side)), dma((2, side)), dma((3, 8)), dma((3, 8)),
-            dma((3, count, side)), dma((3, count, side)), dma((3, count)), dma((3, count)),
-            dma((3, count, nx)), dma((3, count, nx)), dma((2, count, nx)), dma((2, count, nx)),
-            dma((2, count)), dma((2, count)), dma((2, count, side)), dma((2, count, side)),
-            dma((2, 8)), dma((2, 8)),
+            vmem((2, 2, tok, width), BF16), vmem((2, tok, width), BF16),
+            dma((12,)), dma((2,)), dma((2,)), dma((3, 8)), dma((3, 8)),
+            dma((3, count)), dma((3, count)), dma((3, count)), dma((3, count)),
+            dma((3, count)), dma((3, count)), dma((2, count)), dma((2, count)),
+            dma((2, count)), dma((2, count)), dma((2, count, 2)), dma((2, count, 2)),
+            dma((2, 2, 8)), dma((2, 2, 8)),
         ]
         any_spec = pl.BlockSpec(memory_space=pl.ANY)
-        vmem_spec = pl.BlockSpec(memory_space=pltpu.VMEM)
-        out = jax.ShapeDtypeStruct((tok, width), BF16)
-        return pl.pallas_call(
+        out = jax.ShapeDtypeStruct((2, tok, width), BF16)
+        results = pl.pallas_call(
             functools.partial(kernel, side, nx, chunks, tile),
-            out_shape=(out, out),
+            out_shape=out,
             in_specs=[any_spec] * 9,
-            out_specs=(vmem_spec, vmem_spec),
+            out_specs=any_spec,
             scratch_shapes=scratch,
             compiler_params=pltpu.CompilerParams(
                 collective_id=0, has_side_effects=True, vmem_limit_bytes=60 * 2**20
             ),
             cost_estimate=pl.CostEstimate(flops=12 * rows * width * ff, bytes_accessed=6 * width * ff, transcendentals=0),
         )(ft, fi.T, fg.T, bt, bi.T, bg.T, bc, w_up[0], w_down[0])
+        return results[0], results[1]
 
     in_specs = (
         P("expert", "pipe"), P("expert", None), P("expert", None),

time: 132 us -> 123 us (0.932)
  Pallas kernels: 128 us -> 119 us
  local copies, waits for them, and re-layouts: 3.11 us -> 1.66 us
    pallas_call x1, Pallas kernels: 128 us -> 119 us  [local(): pl.pallas_call(functools.partial(kernel, side, nx, chunks, tile), out_sha...]
    unnamed x2 -> x0, local copies, waits for them, and re-layouts: 3.11 us -> none
    squeeze x0 -> x1, local copies, waits for them, and re-layouts: none -> 1.66 us  [local(): return (results[0], results[1])]
where the time goes in v3:
time: 123 us; the launch traced here: 121 us
  Pallas kernels  119 us (97%)
  local copies, waits for them, and re-layouts  1.66 us (1%)
    pallas_call x1, Pallas kernels, local(): pl.pallas_call(functools.partial(kernel, side, nx, chunks, tile), out_sha...  119 us

profile of v3, /device:TPU:6, one launch (start us, length us, event | category | flops | bytes accessed | tf_op | source)
XLA Modules:
  0.0 121.4 jit_solution(5205348855380415257)
XLA Ops:
  0.6 119.1 %shard_map.104 = bf16[2,64,896]{2,1,0:T(8,128)(2,1)} custom-call(bf16[64,896]{1,0:T(8,128)(2,1)} %ft.1, s32[8,64]{1,0:T(8,128)} %bitcast.12, f32[8,64]{1,0:T(8,128)} %bitcast.13, bf16[64,896]{1,0:T(8,128)(2,1)} %bt.1, s32[8,64]{1,0:T(8,128)} %bitcast.14, f32[8,64]{1,0:T(8,128)} %bitcast.15, bf16[64,896]{1,0:T(8,128)(2,1)} %bc.1, bf16[896,1024]{1,0:T(8,128)(2,1)} %bitcast.10, ...), custom_call_target="tpu_custom_call" | custom-call | flops 7046430720 | bytes 5505024 | tf_op jit(solution)/shard_map/pallas_call | solution.py:597
  119.8 1.7 %slice_bitcast_fusion = (bf16[64,896]{1,0:T(8,128)(2,1)}, bf16[64,896]{1,0:T(8,128)(2,1)}) fusion(bf16[2,64,896]{2,1,0:T(8,128)(2,1)} %shard_map.104), kind=kLoop, calls=%fused_computation | loop fusion | bytes 458752 | tf_op jit(solution)/shard_map/squeeze | solution.py:608

commit v4 on v3

--- a/solution.py
+++ b/solution.py
@@ -118,6 +118,8 @@
         (-2, 1, None), (2, -1, None), (-2, 2, 0), (2, -2, 1),
     )
 
+    LAST = 4
+
     def gather_copy(q, kind):
         origin, target, piece = GATHER[kind]
         place = around(j, side + origin, side)
@@ -126,7 +128,11 @@
             rows = pl.ds(pl.multiple_of(place * tok + piece * part, part), part)
         here = gathered.at[q, rows]
         source = tokens[q] if origin == 0 else here
-        return remote(source, here, gat_s.at[q, kind], gat_r.at[q, kind], gather_dev(around(j, side + target, side)))
+        return remote(source, here, gat_s.at[q], gat_r.at[q, min(kind, LAST)], gather_dev(around(j, side + target, side)))
+
+    def gather_copies(q, count):
+        rows = gathered.at[q, pl.ds(0, count)]
+        return remote(rows, rows, gat_s.at[q], gat_r.at[q, LAST], gather_dev(around(j, 1, side)))
 
     def info_copy(r, k):
         there = around(j, k, side)
@@ -200,7 +206,11 @@
             source = part_send.at[r, pl.ds(pl.multiple_of(place * tok + piece * part, part), part), at]
             there = part_recv.at[r, kind, pl.ds(piece * part, part), at]
         device = gather_dev(around(j, side + target, side))
-        return remote(source, there, red_s.at[r, h, kind], red_r.at[r, h, kind], device)
+        return remote(source, there, red_s.at[r, h], red_r.at[r, h, int(2 <= kind < 6)], device)
+
+    def reduce_copies(r, h, early, count):
+        rows = part_send.at[r, pl.ds(0, count), pl.ds(*reduce_spans(r)[h])]
+        return remote(rows, rows, red_s.at[r, h], red_r.at[r, h, early], gather_dev(around(j, 1, side)))
 
     def out_copy(r, h):
         at = pl.ds(*reduce_spans(r)[h])
@@ -330,8 +340,7 @@
 
     def await_gather(q):
         own_block(q).wait()
-        for kind in (4, 5, 6, 7):
-            gather_copy(q, kind).wait_recv()
+        gather_copies(q, 3 * tok).wait_recv()
 
     def dispatch(q, n):
         r = route_of[q]
@@ -449,8 +458,7 @@
                 reduce_copy(r, h, kind).start()
 
     def fold_in(r, h):
-        for kind in (2, 3, 4, 5):
-            reduce_copy(r, h, kind).wait_recv()
+        reduce_copies(r, h, 1, 3 * tok).wait_recv()
         at = pl.ds(*reduce_spans(r)[h])
         for place, owner in enumerate((2, -2)):
             start = around(j, side + owner, side) * tok
@@ -466,16 +474,15 @@
     def finish(r, h):
         at = pl.ds(*reduce_spans(r)[h])
         total = partial[r, block(j), at]
+        reduce_copies(r, h, 0, 4 * tok).wait_recv()
         for kind in (0, 1, 6, 7):
-            reduce_copy(r, h, kind).wait_recv()
             total = total + part_recv[r, kind, :, at].astype(F32)
         result[r, :, at] = total.astype(BF16)
         out_copy(r, h).start()
 
     def drain():
         for q in range(3):
-            for kind in range(8):
-                gather_copy(q, kind).wait_send()
+            gather_copies(q, 7 * tok).wait_send()
             for n in range(len(chunks)):
                 row_copies(q, n).wait_send()
                 pair_copy(q, n).wait_send()
@@ -527,8 +534,8 @@
     share_act(0, 1)
     expand(0, 1)
     project(1, 1)
+    activate(1, 0)
     scatter(1, 1)
-    activate(1, 0)
     project(2, 1)
     scatter(2, 1)
     share_act(1, 0)
@@ -552,8 +559,7 @@
 
     for r in range(2):
         for h in range(len(reduce_spans(r))):
-            for kind in range(8):
-                reduce_copy(r, h, kind).wait_send()
+            reduce_copies(r, h, 0, 7 * tok).wait_send()
             out_copy(r, h).wait()
 
 
@@ -586,11 +592,11 @@
             vmem((rows, width), F32), vmem((2, rows, width), BF16), vmem((2, rows, width), BF16),
             vmem((2, ring, width), F32), vmem((2, ring, width), BF16), vmem((2, 8, tok, width), BF16),
             vmem((2, 2, tok, width), BF16), vmem((2, tok, width), BF16),
-            dma((12,)), dma((2,)), dma((2,)), dma((3, 8)), dma((3, 8)),
+            dma((12,)), dma((2,)), dma((2,)), dma((3,)), dma((3, 5)),
             dma((3, count)), dma((3, count)), dma((3, count)), dma((3, count)),
             dma((3, count)), dma((3, count)), dma((2, count)), dma((2, count)),
             dma((2, count)), dma((2, count)), dma((2, count, 2)), dma((2, count, 2)),
-            dma((2, 2, 8)), dma((2, 2, 8)),
+            dma((2, 2)), dma((2, 2, 2)),
         ]
         any_spec = pl.BlockSpec(memory_space=pl.ANY)
         out = jax.ShapeDtypeStruct((2, tok, width), BF16)

time: 123 us -> 120 us (0.976); the launches traced: 121 us -> 120 us
    pallas_call x1, Pallas kernels: 119 us -> 118 us  [local(): pl.pallas_call(functools.partial(kernel, side, nx, chunks, tile), out_sha...]
where the time goes in v4:
time: 120 us
  Pallas kernels  118 us (98%)
  local copies, waits for them, and re-layouts  1.66 us (1%)
    pallas_call x1, Pallas kernels, local(): pl.pallas_call(functools.partial(kernel, side, nx, chunks, tile), out_sha...  118 us

profile of v4, /device:TPU:6, one launch (start us, length us, event | category | flops | bytes accessed | tf_op | source)
XLA Modules:
  0.0 120.1 jit_solution(14779016490615331828)
XLA Ops:
  0.6 117.8 %shard_map.104 = bf16[2,64,896]{2,1,0:T(8,128)(2,1)} custom-call(bf16[64,896]{1,0:T(8,128)(2,1)} %ft.1, s32[8,64]{1,0:T(8,128)} %bitcast.12, f32[8,64]{1,0:T(8,128)} %bitcast.13, bf16[64,896]{1,0:T(8,128)(2,1)} %bt.1, s32[8,64]{1,0:T(8,128)} %bitcast.14, f32[8,64]{1,0:T(8,128)} %bitcast.15, bf16[64,896]{1,0:T(8,128)(2,1)} %bc.1, bf16[896,1024]{1,0:T(8,128)(2,1)} %bitcast.10, ...), custom_call_target="tpu_custom_call" | custom-call | flops 7046430720 | bytes 5505024 | tf_op jit(solution)/shard_map/pallas_call | solution.py:603
  118.4 1.7 %slice_bitcast_fusion = (bf16[64,896]{1,0:T(8,128)(2,1)}, bf16[64,896]{1,0:T(8,128)(2,1)}) fusion(bf16[2,64,896]{2,1,0:T(8,128)(2,1)} %shard_map.104), kind=kLoop, calls=%fused_computation | loop fusion | bytes 458752 | tf_op jit(solution)/shard_map/squeeze | solution.py:614

commit v5 on v4

--- a/solution.py
+++ b/solution.py
@@ -623,4 +623,4 @@
 
 
 def solution(mesh):
-    return build(mesh, 10, ((0, 48), (48, 32)))
+    return build(mesh, 10, ((0, 32), (32, 48)))

time: 120 us -> 123 us (1.025)
  Pallas kernels: 118 us -> 120 us
    pallas_call x1, Pallas kernels: 118 us -> 120 us  [local(): pl.pallas_call(functools.partial(kernel, side, nx, chunks, tile), out_sha...]
where the time goes in v5:
time: 123 us; the launch traced here: 122 us
  Pallas kernels  120 us (98%)
  local copies, waits for them, and re-layouts  1.66 us (1%)
    pallas_call x1, Pallas kernels, local(): pl.pallas_call(functools.partial(kernel, side, nx, chunks, tile), out_sha...  120 us

profile of v5, /device:TPU:6, one launch (start us, length us, event | category | flops | bytes accessed | tf_op | source)
XLA Modules:
  0.0 122.4 jit_solution(2011633386088442130)
XLA Ops:
  0.6 120.1 %shard_map.104 = bf16[2,64,896]{2,1,0:T(8,128)(2,1)} custom-call(bf16[64,896]{1,0:T(8,128)(2,1)} %ft.1, s32[8,64]{1,0:T(8,128)} %bitcast.12, f32[8,64]{1,0:T(8,128)} %bitcast.13, bf16[64,896]{1,0:T(8,128)(2,1)} %bt.1, s32[8,64]{1,0:T(8,128)} %bitcast.14, f32[8,64]{1,0:T(8,128)} %bitcast.15, bf16[64,896]{1,0:T(8,128)(2,1)} %bc.1, bf16[896,1024]{1,0:T(8,128)(2,1)} %bitcast.10, ...), custom_call_target="tpu_custom_call" | custom-call | flops 7046430720 | bytes 5505024 | tf_op jit(solution)/shard_map/pallas_call | solution.py:603
  120.8 1.7 %slice_bitcast_fusion = (bf16[64,896]{1,0:T(8,128)(2,1)}, bf16[64,896]{1,0:T(8,128)(2,1)}) fusion(bf16[2,64,896]{2,1,0:T(8,128)(2,1)} %shard_map.104), kind=kLoop, calls=%fused_computation | loop fusion | bytes 458752 | tf_op jit(solution)/shard_map/squeeze | solution.py:614
